TPU v7x, 32 devices: a whole 2x2x4 slice. The times are simulated.
32 devices in a mesh: wide: 8 (over y, x, core), grp: 4 (over z).
Axes of the slice: x: 2, y: 2, z: 4, core: 2. Of those that a mesh axis runs over, the one named last changes fastest.
Arguments:
- amplitudes: bfloat16 [32, 32, 256, 256], P(None, 'wide', 'grp'), may hold values from -6 to 6
- integrals: bfloat16 [4, 32, 256, 256], P(None, 'grp', 'wide'), may hold values from -0.09375 to 0.09375
- pair_local: int32 [4, 32], replicated, may hold values from 0 to 1, as said below
Outputs:
- cycle_term: bfloat16 [4, 32, 256, 256], P(None, 'wide', 'grp')
Inputs may be any that keep to these rules, and one draw needn't show every extreme that they name: `pair_local`: 1 marks a pair (i, k) of occupied orbitals inside the locality domain, 0 a screened pair.
All inputs are finite; a program needn't handle non-finite values.
Results may differ from a plain program's by a relative error of at most 0.001.
Values may be sent and summed in bfloat16 or wider, within the bound.
A program may use at most 128 MiB of HBM per device.

v0:
```python
import jax
import jax.numpy as jnp
from jax import lax
from jax.sharding import PartitionSpec as P


def body(amplitudes, integrals, pair_local):
    source_slab = lax.all_to_all(integrals, "grp", split_axis=3, concat_axis=1, tiled=True)
    factor = pair_local.astype(jnp.bfloat16)[:, :, None, None]
    masked = lax.all_gather(source_slab, "wide", axis=2, tiled=True) * factor
    partial_cycle = jnp.einsum(
        "ikac,kjcb->ijab", masked, amplitudes, preferred_element_type=jnp.float32
    )
    summed = lax.psum_scatter(partial_cycle, "grp", scatter_dimension=2, tiled=True)
    return summed.astype(jnp.bfloat16)


def solution(mesh):
    in_specs = (P(None, "wide", "grp", None), P(None, "grp", "wide", None), P())
    out_specs = P(None, "wide", "grp", None)
    return jax.shard_map(body, mesh=mesh, in_specs=in_specs, out_specs=out_specs, check_vma=False)
```

profile of v0, /device:TPU:0, one launch (start us, length us, event | category | flops | bytes accessed | tf_op | source)
XLA Modules:
  0.0 203.7 jit_solution(13153627917543283254)
XLA Ops:
  6.5 0.0 copy-start
  6.5 0.0 all-gather.2.cloned.1.call-start
  6.5 3.8 %copy.6 = bf16[4,8,32,256]{2,1,0,3:T(8,128)(2,1)S(1)} copy(bf16[4,8,32,256]{3,2,1,0:T(8,128)(2,1)} %param.4) | data formatting | bytes 1048576 | tf_op args[1]
  10.4 2.2 %reshape.4 = bf16[4,2,32768]{2,1,0:T(2,128)(2,1)S(1)} reshape(bf16[256,4,8,32]{3,2,1,0:T(8,128)(2,1)S(1)} %bitcast.19) | data formatting | bytes 1048576
  12.6 20.6 %all_to_all.18 = bf16[4,2,32768]{2,1,0:T(2,128)(2,1)S(1)} all-to-all(bf16[4,2,32768]{2,1,0:T(2,128)(2,1)S(1)} %reshape.4), channel_id=1, replica_groups=mesh['wide'=8,'grp'=4] {'grp'}, dimensions={0} | all-to-all | bytes 1048576 | tf_op jit(solution)/shard_map/all_to_all | solution.py:8
  33.2 1.1 reshape.5
  34.3 3.4 %copy.7 = bf16[4,4,8,32,64]{4,2,1,0,3:T(8,128)(2,1)} copy(bf16[4,4,8,32,64]{3,2,0,4,1:T(8,128)(2,1)S(1)} %bitcast.18) | data formatting | bytes 1048576 | tf_op jit(solution)/shard_map/all_to_all | solution.py:8
  37.7 0.0 all-gather.2.cloned.1.call-update
  37.7 0.0 reduce-scatter.2.cloned.1.call-start
  37.8 0.0 copy-done
  37.8 53.6 %all-gather.2.cloned.1.call-done = bf16[4,32,256,64]{3,1,0,2:T(8,128)(2,1)} async-done(((bf16[4,32,32,64]{3,1,0,2:T(8,128)(2,1)}), bf16[4,32,256,64]{3,1,0,2:T(8,128)(2,1)}) %all-gather.2.cloned.1.call-update) | async-done | bytes 4194320 | tf_op jit(solution)/shard_map/all_gather | solution.py:10
  91.4 7.2 %multiply_bitcast_fusion = bf16[4,32,256,64,1]{3,1,0,2,4:T(8,128)(2,1)} fusion(bf16[4,32,256,64]{3,1,0,2:T(8,128)(2,1)} %all-gather.2.cloned.1.call-done, bf16[4,32]{1,0:T(4,128)(2,1)S(1)} %convert_element_type.6), kind=kLoop, calls=%fused_computation.2 | loop fusion | flops 2097152 | bytes 8388864 | tf_op jit(solution)/shard_map/mul | solution.py:10
  98.6 19.2 %fusion.4 = f32[4,4,256,256]{3,2,1,0:T(8,128)} fusion(bf16[32,4,64,256]{3,2,1,0:T(8,128)(2,1)} %param.3, bf16[4,32,256,64,1]{3,1,0,2,4:T(8,128)(2,1)} %multiply_bitcast_fusion), kind=kOutput, calls=%fused_computation.5 | convolution fusion | flops 4294967296 | bytes 12582912 | tf_op jit(solution)/shard_map/ikac,kjcb->ijab/dot_general | solution.py:11
  117.8 0.0 reduce-scatter.2.cloned.1.call-update
  117.8 76.9 %reduce-scatter.2.cloned.1.call-done = f32[4,4,64,256]{3,2,1,0:T(8,128)} async-done(((f32[4,4,256,256]{3,2,1,0:T(8,128)}), f32[4,4,64,256]{3,2,1,0:T(8,128)}) %reduce-scatter.2.cloned.1.call-update) | async-done | bytes 1048592 | tf_op jit(solution)/shard_map/reduce_scatter | solution.py:14
  194.7 2.1 %convert_element_type.7 = bf16[4,4,64,256]{3,2,1,0:T(8,128)(2,1)} convert(f32[4,4,64,256]{3,2,1,0:T(8,128)} %reduce-scatter.2.cloned.1.call-done) | non-fusion elementwise | flops 262144 | bytes 1572864 | tf_op jit(solution)/shard_map/convert_element_type | solution.py:15
  (1 shorter events, 0.0 us)
Async XLA Ops:
  6.5 31.2 %copy-start = (s32[4,32]{1,0:T(4,128)S(1)}, s32[4,32]{1,0:T(4,128)}, u32[]{:S(2)}) copy-start(s32[4,32]{1,0:T(4,128)} %param.5) | copy-start | bytes 1540
  6.5 84.8 %all-gather.2.cloned.1.call-start = ((), (), s32[]{:S(2)}) async-start(), calls=%async_computation.2 | async-start | bytes 9437184 | tf_op jit(solution)/shard_map/all_gather | solution.py:10
  37.7 157.0 %reduce-scatter.2.cloned.1.call-start = ((), (), s32[]{:S(2)}) async-start(), calls=%async_computation.3 | async-start | bytes 5242880 | tf_op jit(solution)/shard_map/reduce_scatter | solution.py:14
Sparse Core Ops, SparseCore 0:
  37.8 53.4 all-gather.1
  117.9 76.7 reduce-scatter.1
where the time goes:
time: 204 us
  waiting for transfers between devices  131 us (64%)
  blocking collectives  20.6 us (10%)
  matrix products  19.2 us (9%)
  between operations  13.4 us (7%)
  local copies, waits for them, and re-layouts  10.5 us (5%)
  other arithmetic  9.31 us (5%)
    reduce_scatter x1, waiting for transfers between devices, body(): lax.psum_scatter(partial_cycle, 'grp', scatter_dimension=2, tiled=True)  76.9 us
    all_gather x1, waiting for transfers between devices, body(): masked = lax.all_gather(source_slab, 'wide', axis=2, tiled=True) * factor  53.6 us
    all_to_all x1, blocking collectives, body(): lax.all_to_all(integrals, 'grp', split_axis=3, concat_axis=1, tiled=True)  20.6 us
    dot_general x1, matrix products, body(): jnp.einsum('ikac,kjcb->ijab', masked, amplitudes, preferred_element_type=...  19.2 us
    mul x1, other arithmetic, body(): masked = lax.all_gather(source_slab, 'wide', axis=2, tiled=True) * factor  7.22 us
    unnamed x5, local copies, waits for them, and re-layouts  7.15 us
  transfers between devices with their start and end apart: 2, of which 2 were waited for; matrix products, arithmetic and copies ran while one was open for 0% of the time, Pallas kernels for 0%

commit v1 on v0

v1 whole, which is shorter than its diff:
```python
import functools

import jax
import jax.numpy as jnp
from jax import lax
from jax.experimental import pallas as pl
from jax.experimental.pallas import tpu as pltpu
from jax.sharding import PartitionSpec as P

MESH = pl.DeviceIdType.MESH


def kernel(n, nw, src, t_hbm, out, t_ref, gath, part, rs_in, t_sem,
           a2a_send, a2a_recv, xy_send, xy_recv, sib_send, sib_recv, rs_send, rs_recv):
    g, w = lax.axis_index("grp"), lax.axis_index("wide")
    chip, core = w // 2, w % 2
    chips = nw // 2
    sibling = chip * 2 + (1 - core)
    rows = src.shape[1]
    k_own = t_ref.shape[0] // n

    t_copy = pltpu.make_async_copy(t_hbm, t_ref, t_sem)
    t_copy.start()

    barrier = pltpu.get_barrier_semaphore()
    for off in range(1, n):
        pl.semaphore_signal(barrier, inc=1, device_id={"grp": (g + off) % n}, device_id_type=MESH)
    for off in range(1, chips):
        pl.semaphore_signal(barrier, inc=1, device_id={"wide": (w + 2 * off) % nw}, device_id_type=MESH)
    pl.semaphore_signal(barrier, inc=1, device_id={"wide": sibling}, device_id_type=MESH)
    pl.semaphore_wait(barrier, n - 1 + chips - 1 + 1)

    def a2a(i, target, source):
        return pltpu.make_async_remote_copy(
            src_ref=src.at[target, i], dst_ref=gath.at[i, w, source],
            send_sem=a2a_send.at[i, target], recv_sem=a2a_recv.at[i, source],
            device_id={"grp": target}, device_id_type=MESH)

    def across(i, target, owner):
        return pltpu.make_async_remote_copy(
            src_ref=gath.at[i, owner], dst_ref=gath.at[i, owner],
            send_sem=xy_send.at[i, target // 2], recv_sem=xy_recv.at[i, owner // 2],
            device_id={"wide": target}, device_id_type=MESH)

    def to_sibling(i, owner):
        return pltpu.make_async_remote_copy(
            src_ref=gath.at[i, owner], dst_ref=gath.at[i, owner],
            send_sem=sib_send.at[i, owner // 2], recv_sem=sib_recv.at[i, owner // 2],
            device_id={"wide": sibling}, device_id_type=MESH)

    def chain(i, dest, way):
        return pltpu.make_async_remote_copy(
            src_ref=part.at[i, dest], dst_ref=rs_in.at[way, i, dest],
            send_sem=rs_send.at[way, i, dest], recv_sem=rs_recv.at[way, i, dest],
            device_id={"grp": (g + 1) % n if way == 0 else (g + n - 1) % n}, device_id_type=MESH)

    @pl.loop(0, rows)
    def _(i):
        for off in range(1, n):
            a2a(i, (g + off) % n, g).start()

    gath[:, w, g] = src[g]

    def forward(i):
        for off in range(1, n):
            a2a(i, g, (g + off) % n).wait_recv()
        for off in range(1, chips):
            across(i, (w + 2 * off) % nw, w).start()
        to_sibling(i, w).start()

    def spread(i):
        for off in range(1, chips):
            owner = (w + 2 * off) % nw
            across(i, w, owner).wait_recv()
            to_sibling(i, owner).start()

    def compute(i):
        for c in range(chips):
            to_sibling(i, c * 2 + (1 - core)).wait_recv()

        @pl.loop(0, t_ref.shape[1])
        def _(j):
            acc = None
            for z in range(n):
                left = gath[i, :, z]
                left = left.reshape(left.shape[0] * left.shape[1], left.shape[2])
                right = t_ref[z * k_own:(z + 1) * k_own, j]
                right = right.reshape(right.shape[0] * right.shape[1], right.shape[2])
                term = jnp.dot(left, right, preferred_element_type=jnp.float32)
                acc = term if acc is None else acc + term
            part[i, :, j] = acc.reshape(part.shape[1], part.shape[3], part.shape[4])

    def sources(i):
        @pl.when(g == 0)
        def _():
            @pl.loop(0, n - 1)
            def _(s):
                chain(i, n - 1 - s, 0).start()

        @pl.when(g == n - 1)
        def _():
            @pl.loop(0, n - 1)
            def _(d):
                chain(i, d, 1).start()

    def relay(i):
        @pl.loop(0, n - 1)
        def _(s):
            d = n - 1 - s

            @pl.when((g > 0) & (d > g))
            def _():
                chain(i, d, 0).wait_recv()
                part[i, d] += rs_in[0, i, d]
                chain(i, d, 0).start()

            e = s

            @pl.when((g < n - 1) & (e < g))
            def _():
                chain(i, e, 1).wait_recv()
                part[i, e] += rs_in[1, i, e]
                chain(i, e, 1).start()

    def finish(i):
        @pl.when(g > 0)
        def _():
            chain(i, g, 0).wait_recv()
            part[i, g] += rs_in[0, i, g]

        @pl.when(g < n - 1)
        def _():
            chain(i, g, 1).wait_recv()
            part[i, g] += rs_in[1, i, g]

        out[i] = part[i, g].astype(out.dtype)

    forward(0)

    @pl.loop(0, rows)
    def _(i):
        spread(i)

        @pl.when(i + 1 < rows)
        def _():
            forward(i + 1)

        @pl.when(i == 0)
        def _():
            t_copy.wait()

        compute(i)
        sources(i)

        @pl.when(i > 0)
        def _():
            relay(i - 1)

    relay(rows - 1)

    @pl.loop(0, rows)
    def _(i):
        finish(i)

    @pl.loop(0, rows)
    def _(i):
        for off in range(1, n):
            a2a(i, (g + off) % n, g).wait_send()
        for off in range(1, chips):
            across(i, (w + 2 * off) % nw, w).wait_send()
        for c in range(chips):
            to_sibling(i, c * 2 + core).wait_send()

        @pl.loop(0, n)
        def _(d):
            @pl.when(d > g)
            def _():
                chain(i, d, 0).wait_send()

            @pl.when(d < g)
            def _():
                chain(i, d, 1).wait_send()


def body(n, nw, amplitudes, integrals, pair_local):
    rows, k_own, a_own, v = integrals.shape
    c_own = v // n
    g = lax.axis_index("grp")
    mine = lax.dynamic_slice_in_dim(pair_local, g * k_own, k_own, 1)
    masked = integrals * mine.astype(jnp.bfloat16)[:, :, None, None]
    blocks = masked.reshape(rows, k_own, a_own, n, c_own).transpose(3, 0, 2, 1, 4)
    blocks = blocks.reshape(n, rows, a_own, k_own * c_own)
    occ, j_own, _, b = amplitudes.shape
    a_out = a_own * nw // n
    chips = nw // 2
    dma = pltpu.SemaphoreType.DMA
    return pl.pallas_call(
        functools.partial(kernel, n, nw),
        out_shape=jax.ShapeDtypeStruct((rows, j_own, a_out, b), jnp.bfloat16),
        in_specs=[pl.BlockSpec(memory_space=pltpu.VMEM), pl.BlockSpec(memory_space=pl.ANY)],
        out_specs=pl.BlockSpec(memory_space=pltpu.VMEM),
        scratch_shapes=[
            pltpu.VMEM(amplitudes.shape, jnp.bfloat16),
            pltpu.VMEM((rows, nw, n, a_own, k_own * c_own), jnp.bfloat16),
            pltpu.VMEM((rows, n, j_own, a_out, b), jnp.float32),
            pltpu.VMEM((2, rows, n, j_own, a_out, b), jnp.float32),
            dma,
            dma((rows, n)), dma((rows, n)),
            dma((rows, chips)), dma((rows, chips)),
            dma((rows, chips)), dma((rows, chips)),
            dma((2, rows, n)), dma((2, rows, n)),
        ],
        compiler_params=pltpu.CompilerParams(
            collective_id=0, has_side_effects=True, vmem_limit_bytes=48 * 1024 * 1024),
        cost_estimate=pl.CostEstimate(
            flops=2 * rows * j_own * v * b * occ * c_own,
            bytes_accessed=2 * amplitudes.size, transcendentals=0),
    )(blocks, amplitudes)


def solution(mesh):
    in_specs = (P(None, "wide", "grp", None), P(None, "grp", "wide", None), P())
    out_specs = P(None, "wide", "grp", None)
    fn = functools.partial(body, mesh.shape["grp"], mesh.shape["wide"])
    return jax.shard_map(fn, mesh=mesh, in_specs=in_specs, out_specs=out_specs, check_vma=False)
```

time: 204 us -> 117 us (0.57)
  waiting for transfers between devices: 131 us -> 0 us
  Pallas kernels: 0 us -> 110 us
  blocking collectives: 20.6 us -> 0 us
  matrix products: 19.2 us -> 0 us
  between operations: 13.4 us -> 0.05 us
  other arithmetic: 9.31 us -> 1.9 us
  local copies, waits for them, and re-layouts: 10.5 us -> 4.67 us
    pallas_call x0 -> x1, Pallas kernels: none -> 110 us  [body(): pl.pallas_call(functools.partial(kernel, n, nw), out_shape=jax.ShapeDtype...]
    reduce_scatter x1 -> x0, waiting for transfers between devices: 76.9 us -> none  [body(): lax.psum_scatter(partial_cycle, 'grp', scatter_dimension=2, tiled=True)]
    all_gather x1 -> x0, waiting for transfers between devices: 53.6 us -> none  [body(): masked = lax.all_gather(source_slab, 'wide', axis=2, tiled=True) * factor]
    all_to_all x1 -> x0, blocking collectives: 20.6 us -> none  [body(): lax.all_to_all(integrals, 'grp', split_axis=3, concat_axis=1, tiled=True)]
    dot_general x1 -> x0, matrix products: 19.2 us -> none  [body(): jnp.einsum('ikac,kjcb->ijab', masked, amplitudes, preferred_element_type=...]
    mul x1, other arithmetic: 7.22 us -> 1.14 us  [body(): masked = integrals * mine.astype(jnp.bfloat16)[:, :, None, None]]
    unnamed x5 -> x3, local copies, waits for them, and re-layouts: 7.15 us -> 2.98 us
    all_to_all x1 -> x0, local copies, waits for them, and re-layouts: 3.36 us -> none  [body(): lax.all_to_all(integrals, 'grp', split_axis=3, concat_axis=1, tiled=True)]
  transfers between devices with their start and end apart: 2 -> 0, of which waited for: 2 -> 0; matrix products, arithmetic and copies ran while one was open for 0% -> 0% of each run, Pallas kernels for 0% -> 0%
where the time goes in v1:
time: 117 us
  Pallas kernels  110 us (94%)
  local copies, waits for them, and re-layouts  4.67 us (4%)
  other arithmetic  1.9 us (2%)
    pallas_call x1, Pallas kernels, body(): pl.pallas_call(functools.partial(kernel, n, nw), out_shape=jax.ShapeDtype...  110 us
    unnamed x3, local copies, waits for them, and re-layouts  2.98 us

profile of v1, /device:TPU:0, one launch (start us, length us, event | category | flops | bytes accessed | tf_op | source)
XLA Modules:
  0.0 116.6 jit_solution(8422681023357984434)
XLA Ops:
  0.0 0.8 dynamic-slice_convert_fusion
  0.8 1.1 broadcast_multiply_fusion
  1.9 0.4 reshape.7
  2.3 0.7 copy.6
  3.0 0.6 reshape.8.src
  3.6 0.0 copy-start
  3.6 2.2 %copy-done = bf16[32,4,64,256]{3,2,1,0:T(8,128)(2,1)S(1)} copy-done((bf16[32,4,64,256]{3,2,1,0:T(8,128)(2,1)S(1)}, bf16[32,4,64,256]{3,2,1,0:T(8,128)(2,1)}, u32[]{:S(2)}) %copy-start) | copy-done | bytes 4194328
  5.8 110.0 %shard_map.37 = bf16[4,4,64,256]{3,2,1,0:T(8,128)(2,1)S(1)} custom-call(bf16[4,4,32,512]{3,2,1,0:T(8,128)(2,1)S(1)} %reshape.8.src, bf16[32,4,64,256]{3,2,1,0:T(8,128)(2,1)S(1)} %copy-done), custom_call_target="tpu_custom_call" | custom-call | flops 4294967296 | bytes 4194304 | tf_op jit(solution)/shard_map/pallas_call | solution.py:197
  115.8 0.8 copy.8
Async XLA Ops:
  3.6 2.2 %copy-start = (bf16[32,4,64,256]{3,2,1,0:T(8,128)(2,1)S(1)}, bf16[32,4,64,256]{3,2,1,0:T(8,128)(2,1)}, u32[]{:S(2)}) copy-start(bf16[32,4,64,256]{3,2,1,0:T(8,128)(2,1)} %t_hbm.1) | copy-start | bytes 12582916

commit v2 on v1

--- a/solution.py
+++ b/solution.py
@@ -10,17 +10,52 @@
 MESH = pl.DeviceIdType.MESH
 
 
-def kernel(n, nw, src, t_hbm, out, t_ref, gath, part, rs_in, t_sem,
-           a2a_send, a2a_recv, xy_send, xy_recv, sib_send, sib_recv, rs_send, rs_recv):
+STEPS = 127.0 * 256.0
+
+
+def encode(x):
+    head = x.astype(jnp.bfloat16)
+    wide = head.astype(jnp.float32)
+    zero = wide == 0.0
+    ratio = jnp.where(zero, 0.0, (x - wide) / jnp.where(zero, 1.0, wide))
+    steps = jnp.round(ratio * STEPS)
+    half = x.shape[0] // 2
+    tail = steps[:half] * 256.0 + (steps[half:] + 128.0)
+    return head, tail.astype(jnp.int32).astype(jnp.int16)
+
+
+def decode(head, tail):
+    both = tail.astype(jnp.int32).astype(jnp.float32)
+    upper = jnp.floor(both * (1.0 / 256.0))
+    lower = both - upper * 256.0 - 128.0
+    wide = head.astype(jnp.float32)
+    half = head.shape[0] // 2
+    return (wide[:half] + wide[:half] * (upper * (1.0 / STEPS)),
+            wide[half:] + wide[half:] * (lower * (1.0 / STEPS)))
+
+
+def kernel(n, nw, pairs, w_ref, t_hbm, out, src, t_ref, gath, part, head_out, tail_out, head_in, tail_in,
+           t_sem, a2a_send, a2a_recv, xy_send, xy_recv, sib_send, sib_recv,
+           head_send, head_recv, tail_send, tail_recv):
     g, w = lax.axis_index("grp"), lax.axis_index("wide")
     chip, core = w // 2, w % 2
     chips = nw // 2
     sibling = chip * 2 + (1 - core)
-    rows = src.shape[1]
+    rows, k_here, _, v = w_ref.shape
+    c_own = v // n
+    half = t_ref.shape[1] // 2
     k_own = t_ref.shape[0] // n
 
     t_copy = pltpu.make_async_copy(t_hbm, t_ref, t_sem)
     t_copy.start()
+
+    def prepare(i):
+        masked = [w_ref[i, k].astype(jnp.float32) * pairs[i, g * k_here + k].astype(jnp.float32)
+                  for k in range(k_here)]
+        for target in range(n):
+            block = [m[:, target * c_own:(target + 1) * c_own] for m in masked]
+            src[target, i] = jnp.concatenate(block, axis=1).astype(src.dtype)
+        gath[i, w, g] = src[g, i]
 
     barrier = pltpu.get_barrier_semaphore()
     for off in range(1, n):
@@ -28,6 +63,7 @@
     for off in range(1, chips):
         pl.semaphore_signal(barrier, inc=1, device_id={"wide": (w + 2 * off) % nw}, device_id_type=MESH)
     pl.semaphore_signal(barrier, inc=1, device_id={"wide": sibling}, device_id_type=MESH)
+    prepare(0)
     pl.semaphore_wait(barrier, n - 1 + chips - 1 + 1)
 
     def a2a(i, target, source):
@@ -48,18 +84,45 @@
             send_sem=sib_send.at[i, owner // 2], recv_sem=sib_recv.at[i, owner // 2],
             device_id={"wide": sibling}, device_id_type=MESH)
 
-    def chain(i, dest, way):
-        return pltpu.make_async_remote_copy(
-            src_ref=part.at[i, dest], dst_ref=rs_in.at[way, i, dest],
-            send_sem=rs_send.at[way, i, dest], recv_sem=rs_recv.at[way, i, dest],
-            device_id={"grp": (g + 1) % n if way == 0 else (g + n - 1) % n}, device_id_type=MESH)
-
-    @pl.loop(0, rows)
-    def _(i):
+    class chain:
+        def __init__(self, i, dest, way):
+            to = {"grp": (g + 1) % n if way == 0 else (g + n - 1) % n}
+            self.at = (i, dest)
+            self.into = (way, i, dest)
+            self.copies = [
+                pltpu.make_async_remote_copy(
+                    src_ref=box.at[i, dest], dst_ref=slot.at[way, i, dest],
+                    send_sem=sent.at[way, i, dest], recv_sem=came.at[way, i, dest],
+                    device_id=to, device_id_type=MESH)
+                for box, slot, sent, came in (
+                    (head_out, head_in, head_send, head_recv), (tail_out, tail_in, tail_send, tail_recv))]
+
+        def start(self):
+            head_out[self.at], tail_out[self.at] = encode(part[self.at])
+            for copy in self.copies:
+                copy.start()
+
+        def add(self):
+            for copy in self.copies:
+                copy.wait_recv()
+            low, high = decode(head_in[self.into], tail_in[self.into])
+            i, dest = self.at
+            part[i, dest, :half] += low
+            part[i, dest, half:] += high
+
+        def wait_send(self):
+            for copy in self.copies:
+                copy.wait_send()
+
+    def exchange(i):
         for off in range(1, n):
             a2a(i, (g + off) % n, g).start()
 
-    gath[:, w, g] = src[g]
+    exchange(0)
+
+    @pl.loop(1, rows)
+    def _(i):
+        prepare(i)
 
     def forward(i):
         for off in range(1, n):
@@ -110,32 +173,32 @@
 
             @pl.when((g > 0) & (d > g))
             def _():
-                chain(i, d, 0).wait_recv()
-                part[i, d] += rs_in[0, i, d]
+                chain(i, d, 0).add()
                 chain(i, d, 0).start()
 
             e = s
 
             @pl.when((g < n - 1) & (e < g))
             def _():
-                chain(i, e, 1).wait_recv()
-                part[i, e] += rs_in[1, i, e]
+                chain(i, e, 1).add()
                 chain(i, e, 1).start()
 
     def finish(i):
         @pl.when(g > 0)
         def _():
-            chain(i, g, 0).wait_recv()
-            part[i, g] += rs_in[0, i, g]
+            chain(i, g, 0).add()
 
         @pl.when(g < n - 1)
         def _():
-            chain(i, g, 1).wait_recv()
-            part[i, g] += rs_in[1, i, g]
+            chain(i, g, 1).add()
 
         out[i] = part[i, g].astype(out.dtype)
 
     forward(0)
+
+    @pl.loop(1, rows)
+    def _(i):
+        exchange(i)
 
     @pl.loop(0, rows)
     def _(i):
@@ -156,10 +219,12 @@
         def _():
             relay(i - 1)
 
+        @pl.when(i > 1)
+        def _():
+            finish(i - 2)
+
     relay(rows - 1)
-
-    @pl.loop(0, rows)
-    def _(i):
+    for i in range(max(rows - 2, 0), rows):
         finish(i)
 
     @pl.loop(0, rows)
@@ -185,11 +250,6 @@
 def body(n, nw, amplitudes, integrals, pair_local):
     rows, k_own, a_own, v = integrals.shape
     c_own = v // n
-    g = lax.axis_index("grp")
-    mine = lax.dynamic_slice_in_dim(pair_local, g * k_own, k_own, 1)
-    masked = integrals * mine.astype(jnp.bfloat16)[:, :, None, None]
-    blocks = masked.reshape(rows, k_own, a_own, n, c_own).transpose(3, 0, 2, 1, 4)
-    blocks = blocks.reshape(n, rows, a_own, k_own * c_own)
     occ, j_own, _, b = amplitudes.shape
     a_out = a_own * nw // n
     chips = nw // 2
@@ -197,25 +257,31 @@
     return pl.pallas_call(
         functools.partial(kernel, n, nw),
         out_shape=jax.ShapeDtypeStruct((rows, j_own, a_out, b), jnp.bfloat16),
-        in_specs=[pl.BlockSpec(memory_space=pltpu.VMEM), pl.BlockSpec(memory_space=pl.ANY)],
+        in_specs=[pl.BlockSpec(memory_space=pltpu.SMEM), pl.BlockSpec(memory_space=pltpu.VMEM),
+                  pl.BlockSpec(memory_space=pl.ANY)],
         out_specs=pl.BlockSpec(memory_space=pltpu.VMEM),
         scratch_shapes=[
+            pltpu.VMEM((n, rows, a_own, k_own * c_own), jnp.bfloat16),
             pltpu.VMEM(amplitudes.shape, jnp.bfloat16),
             pltpu.VMEM((rows, nw, n, a_own, k_own * c_own), jnp.bfloat16),
             pltpu.VMEM((rows, n, j_own, a_out, b), jnp.float32),
-            pltpu.VMEM((2, rows, n, j_own, a_out, b), jnp.float32),
+            pltpu.VMEM((rows, n, j_own, a_out, b), jnp.bfloat16),
+            pltpu.VMEM((rows, n, j_own // 2, a_out, b), jnp.int16),
+            pltpu.VMEM((2, rows, n, j_own, a_out, b), jnp.bfloat16),
+            pltpu.VMEM((2, rows, n, j_own // 2, a_out, b), jnp.int16),
             dma,
             dma((rows, n)), dma((rows, n)),
             dma((rows, chips)), dma((rows, chips)),
             dma((rows, chips)), dma((rows, chips)),
             dma((2, rows, n)), dma((2, rows, n)),
+            dma((2, rows, n)), dma((2, rows, n)),
         ],
         compiler_params=pltpu.CompilerParams(
-            collective_id=0, has_side_effects=True, vmem_limit_bytes=48 * 1024 * 1024),
+            collective_id=0, has_side_effects=True, vmem_limit_bytes=60 * 1024 * 1024),
         cost_estimate=pl.CostEstimate(
             flops=2 * rows * j_own * v * b * occ * c_own,
             bytes_accessed=2 * amplitudes.size, transcendentals=0),
-    )(blocks, amplitudes)
+    )(pair_local, integrals, amplitudes)
 
 
 def solution(mesh):

time: 117 us -> 104 us (0.89)
  Pallas kernels: 110 us -> 102 us
  local copies, waits for them, and re-layouts: 4.67 us -> 1.88 us
  other arithmetic: 1.9 us -> 0 us
    pallas_call x1, Pallas kernels: 110 us -> 102 us  [body(): pl.pallas_call(functools.partial(kernel, n, nw), out_shape=jax.ShapeDtype...]
    reshape x3 -> x0, local copies, waits for them, and re-layouts: 1.69 us -> none  [the longest x2 1.09 us: body(): masked.reshape(rows, k_own, a_own, n, c_own).transpose(3, 0, 2, 1, 4)]
    unnamed x3 -> x1, local copies, waits for them, and re-layouts: 2.98 us -> 1.88 us
where the time goes in v2:
time: 104 us
  Pallas kernels  102 us (98%)
  local copies, waits for them, and re-layouts  1.88 us (2%)
    pallas_call x1, Pallas kernels, body(): pl.pallas_call(functools.partial(kernel, n, nw), out_shape=jax.ShapeDtype...  102 us

profile of v2, /device:TPU:0, one launch (start us, length us, event | category | flops | bytes accessed | tf_op | source)
XLA Modules:
  0.0 103.7 jit_solution(13427242283379541612)
XLA Ops:
  0.0 101.8 %shard_map.37 = bf16[4,4,64,256]{3,2,1,0:T(8,128)(2,1)} custom-call(s32[4,32]{1,0:T(4,128)} %pairs.1, bf16[4,8,32,256]{3,2,1,0:T(8,128)(2,1)} %w_ref.1, bf16[32,4,64,256]{3,2,1,0:T(8,128)(2,1)} %t_hbm.1), custom_call_target="tpu_custom_call" | custom-call | flops 4294967296 | bytes 4194304 | tf_op jit(solution)/shard_map/pallas_call | solution.py:257
  101.8 1.9 %copy.5 = bf16[4,4,64,256]{3,2,1,0:T(8,128)(2,1)} copy(bf16[4,4,64,256]{3,2,1,0:T(8,128)(2,1)} %shard_map.37) | data formatting | bytes 1048576

commit v3 on v2

--- a/solution.py
+++ b/solution.py
@@ -44,10 +44,13 @@
     rows, k_here, _, v = w_ref.shape
     c_own = v // n
     half = t_ref.shape[1] // 2
-    k_own = t_ref.shape[0] // n
+    depth = k_here * c_own
 
     t_copy = pltpu.make_async_copy(t_hbm, t_ref, t_sem)
     t_copy.start()
+
+    def span(rank):
+        return pl.ds(pl.multiple_of(rank * depth, depth), depth)
 
     def prepare(i):
         masked = [w_ref[i, k].astype(jnp.float32) * pairs[i, g * k_here + k].astype(jnp.float32)
@@ -55,7 +58,7 @@
         for target in range(n):
             block = [m[:, target * c_own:(target + 1) * c_own] for m in masked]
             src[target, i] = jnp.concatenate(block, axis=1).astype(src.dtype)
-        gath[i, w, g] = src[g, i]
+        gath[i, w, :, span(g)] = src[g, i]
 
     barrier = pltpu.get_barrier_semaphore()
     for off in range(1, n):
@@ -68,7 +71,7 @@
 
     def a2a(i, target, source):
         return pltpu.make_async_remote_copy(
-            src_ref=src.at[target, i], dst_ref=gath.at[i, w, source],
+            src_ref=src.at[target, i], dst_ref=gath.at[i, w, :, span(source)],
             send_sem=a2a_send.at[i, target], recv_sem=a2a_recv.at[i, source],
             device_id={"grp": target}, device_id_type=MESH)
 
@@ -143,14 +146,11 @@
 
         @pl.loop(0, t_ref.shape[1])
         def _(j):
-            acc = None
-            for z in range(n):
-                left = gath[i, :, z]
-                left = left.reshape(left.shape[0] * left.shape[1], left.shape[2])
-                right = t_ref[z * k_own:(z + 1) * k_own, j]
-                right = right.reshape(right.shape[0] * right.shape[1], right.shape[2])
-                term = jnp.dot(left, right, preferred_element_type=jnp.float32)
-                acc = term if acc is None else acc + term
+            left = gath[i]
+            left = left.reshape(left.shape[0] * left.shape[1], left.shape[2])
+            right = t_ref[:, j]
+            right = right.reshape(right.shape[0] * right.shape[1], right.shape[2])
+            acc = jnp.dot(left, right, preferred_element_type=jnp.float32)
             part[i, :, j] = acc.reshape(part.shape[1], part.shape[3], part.shape[4])
 
     def sources(i):
@@ -167,21 +167,31 @@
                 chain(i, d, 1).start()
 
     def relay(i):
-        @pl.loop(0, n - 1)
-        def _(s):
-            d = n - 1 - s
-
-            @pl.when((g > 0) & (d > g))
-            def _():
-                chain(i, d, 0).add()
-                chain(i, d, 0).start()
-
-            e = s
-
-            @pl.when((g < n - 1) & (e < g))
-            def _():
-                chain(i, e, 1).add()
-                chain(i, e, 1).start()
+        def rightward():
+            @pl.loop(0, n - 1)
+            def _(s):
+                @pl.when((g > 0) & (n - 1 - s > g))
+                def _():
+                    chain(i, n - 1 - s, 0).add()
+                    chain(i, n - 1 - s, 0).start()
+
+        def leftward():
+            @pl.loop(0, n - 1)
+            def _(d):
+                @pl.when((g < n - 1) & (d < g))
+                def _():
+                    chain(i, d, 1).add()
+                    chain(i, d, 1).start()
+
+        @pl.when(g < n // 2)
+        def _():
+            rightward()
+            leftward()
+
+        @pl.when(g >= n // 2)
+        def _():
+            leftward()
+            rightward()
 
     def finish(i):
         @pl.when(g > 0)
@@ -258,12 +268,12 @@
         functools.partial(kernel, n, nw),
         out_shape=jax.ShapeDtypeStruct((rows, j_own, a_out, b), jnp.bfloat16),
         in_specs=[pl.BlockSpec(memory_space=pltpu.SMEM), pl.BlockSpec(memory_space=pltpu.VMEM),
-                  pl.BlockSpec(memory_space=pl.ANY)],
+                  pl.BlockSpec(memory_space=pltpu.HBM)],
         out_specs=pl.BlockSpec(memory_space=pltpu.VMEM),
         scratch_shapes=[
             pltpu.VMEM((n, rows, a_own, k_own * c_own), jnp.bfloat16),
             pltpu.VMEM(amplitudes.shape, jnp.bfloat16),
-            pltpu.VMEM((rows, nw, n, a_own, k_own * c_own), jnp.bfloat16),
+            pltpu.VMEM((rows, nw, a_own, n * k_own * c_own), jnp.bfloat16),
             pltpu.VMEM((rows, n, j_own, a_out, b), jnp.float32),
             pltpu.VMEM((rows, n, j_own, a_out, b), jnp.bfloat16),
             pltpu.VMEM((rows, n, j_own // 2, a_out, b), jnp.int16),
@@ -277,7 +287,7 @@
             dma((2, rows, n)), dma((2, rows, n)),
         ],
         compiler_params=pltpu.CompilerParams(
-            collective_id=0, has_side_effects=True, vmem_limit_bytes=60 * 1024 * 1024),
+            collective_id=0, has_side_effects=True, vmem_limit_bytes=58 * 1024 * 1024),
         cost_estimate=pl.CostEstimate(
             flops=2 * rows * j_own * v * b * occ * c_own,
             bytes_accessed=2 * amplitudes.size, transcendentals=0),

time: 104 us -> 83 us (0.80)
  Pallas kernels: 102 us -> 80.9 us
    pallas_call x1, Pallas kernels: 102 us -> 80.9 us  [body(): pl.pallas_call(functools.partial(kernel, n, nw), out_shape=jax.ShapeDtype...]
where the time goes in v3:
time: 83 us; the launch traced here: 82.8 us
  Pallas kernels  80.9 us (97%)
  local copies, waits for them, and re-layouts  1.88 us (2%)
    pallas_call x1, Pallas kernels, body(): pl.pallas_call(functools.partial(kernel, n, nw), out_shape=jax.ShapeDtype...  80.9 us
    unnamed x1, local copies, waits for them, and re-layouts  1.88 us

profile of v3, /device:TPU:0, one launch (start us, length us, event | category | flops | bytes accessed | tf_op | source)
XLA Modules:
  0.0 82.8 jit_solution(17402503797160523707)
XLA Ops:
  0.0 80.9 %shard_map.37 = bf16[4,4,64,256]{3,2,1,0:T(8,128)(2,1)} custom-call(s32[4,32]{1,0:T(4,128)} %pairs.1, bf16[4,8,32,256]{3,2,1,0:T(8,128)(2,1)} %w_ref.1, bf16[32,4,64,256]{3,2,1,0:T(8,128)(2,1)} %t_hbm.1), custom_call_target="tpu_custom_call" | custom-call | flops 4294967296 | bytes 4194304 | tf_op jit(solution)/shard_map/pallas_call | solution.py:267
  80.9 1.9 %copy.5 = bf16[4,4,64,256]{3,2,1,0:T(8,128)(2,1)} copy(bf16[4,4,64,256]{3,2,1,0:T(8,128)(2,1)} %shard_map.37) | data formatting | bytes 1048576

commit v4 on v3

--- a/solution.py
+++ b/solution.py
@@ -41,7 +41,10 @@
     chip, core = w // 2, w % 2
     chips = nw // 2
     sibling = chip * 2 + (1 - core)
-    rows, k_here, _, v = w_ref.shape
+    rows, k_here, a_own, v = w_ref.shape
+    chunks, a_c = src.shape[1], src.shape[2]
+    split = chunks // rows
+    lag = 2 * split
     c_own = v // n
     half = t_ref.shape[1] // 2
     depth = k_here * c_own
@@ -53,7 +56,8 @@
         return pl.ds(pl.multiple_of(rank * depth, depth), depth)
 
     def prepare(i):
-        masked = [w_ref[i, k].astype(jnp.float32) * pairs[i, g * k_here + k].astype(jnp.float32)
+        row, at = i // split, pl.ds(pl.multiple_of((i % split) * a_c, a_c), a_c)
+        masked = [w_ref[row, k, at].astype(jnp.float32) * pairs[row, g * k_here + k].astype(jnp.float32)
                   for k in range(k_here)]
         for target in range(n):
             block = [m[:, target * c_own:(target + 1) * c_own] for m in masked]
@@ -123,7 +127,7 @@
 
     exchange(0)
 
-    @pl.loop(1, rows)
+    @pl.loop(1, chunks)
     def _(i):
         prepare(i)
 
@@ -202,19 +206,24 @@
         def _():
             chain(i, g, 1).add()
 
-        out[i] = part[i, g].astype(out.dtype)
+        if split == 1:
+            out[i] = part[i, g].astype(out.dtype)
+        else:
+            for p in range(nw // n):
+                at = pl.ds(pl.multiple_of(p * a_own + (i % split) * a_c, a_c), a_c)
+                out[i // split, :, at] = part[i, g, :, p * a_c:(p + 1) * a_c].astype(out.dtype)
 
     forward(0)
 
-    @pl.loop(1, rows)
+    @pl.loop(1, chunks)
     def _(i):
         exchange(i)
 
-    @pl.loop(0, rows)
+    @pl.loop(0, chunks)
     def _(i):
         spread(i)
 
-        @pl.when(i + 1 < rows)
+        @pl.when(i + 1 < chunks)
         def _():
             forward(i + 1)
 
@@ -229,15 +238,17 @@
         def _():
             relay(i - 1)
 
-        @pl.when(i > 1)
-        def _():
-            finish(i - 2)
-
-    relay(rows - 1)
-    for i in range(max(rows - 2, 0), rows):
+        @pl.when(i >= lag)
+        def _():
+            finish(i - lag)
+
+    relay(chunks - 1)
+
+    @pl.loop(max(chunks - lag, 0), chunks)
+    def _(i):
         finish(i)
 
-    @pl.loop(0, rows)
+    @pl.loop(0, chunks)
     def _(i):
         for off in range(1, n):
             a2a(i, (g + off) % n, g).wait_send()
@@ -263,6 +274,8 @@
     occ, j_own, _, b = amplitudes.shape
     a_out = a_own * nw // n
     chips = nw // 2
+    split = 2 if a_own % 32 == 0 else 1
+    chunks, a_c, a_out_c = rows * split, a_own // split, a_out // split
     dma = pltpu.SemaphoreType.DMA
     return pl.pallas_call(
         functools.partial(kernel, n, nw),
@@ -271,23 +284,23 @@
                   pl.BlockSpec(memory_space=pltpu.HBM)],
         out_specs=pl.BlockSpec(memory_space=pltpu.VMEM),
         scratch_shapes=[
-            pltpu.VMEM((n, rows, a_own, k_own * c_own), jnp.bfloat16),
+            pltpu.VMEM((n, chunks, a_c, k_own * c_own), jnp.bfloat16),
             pltpu.VMEM(amplitudes.shape, jnp.bfloat16),
-            pltpu.VMEM((rows, nw, a_own, n * k_own * c_own), jnp.bfloat16),
-            pltpu.VMEM((rows, n, j_own, a_out, b), jnp.float32),
-            pltpu.VMEM((rows, n, j_own, a_out, b), jnp.bfloat16),
-            pltpu.VMEM((rows, n, j_own // 2, a_out, b), jnp.int16),
-            pltpu.VMEM((2, rows, n, j_own, a_out, b), jnp.bfloat16),
-            pltpu.VMEM((2, rows, n, j_own // 2, a_out, b), jnp.int16),
+            pltpu.VMEM((chunks, nw, a_c, n * k_own * c_own), jnp.bfloat16),
+            pltpu.VMEM((chunks, n, j_own, a_out_c, b), jnp.float32),
+            pltpu.VMEM((chunks, n, j_own, a_out_c, b), jnp.bfloat16),
+            pltpu.VMEM((chunks, n, j_own // 2, a_out_c, b), jnp.int16),
+            pltpu.VMEM((2, chunks, n, j_own, a_out_c, b), jnp.bfloat16),
+            pltpu.VMEM((2, chunks, n, j_own // 2, a_out_c, b), jnp.int16),
             dma,
-            dma((rows, n)), dma((rows, n)),
-            dma((rows, chips)), dma((rows, chips)),
-            dma((rows, chips)), dma((rows, chips)),
-            dma((2, rows, n)), dma((2, rows, n)),
-            dma((2, rows, n)), dma((2, rows, n)),
+            dma((chunks, n)), dma((chunks, n)),
+            dma((chunks, chips)), dma((chunks, chips)),
+            dma((chunks, chips)), dma((chunks, chips)),
+            dma((2, chunks, n)), dma((2, chunks, n)),
+            dma((2, chunks, n)), dma((2, chunks, n)),
         ],
         compiler_params=pltpu.CompilerParams(
-            collective_id=0, has_side_effects=True, vmem_limit_bytes=58 * 1024 * 1024),
+            collective_id=0, has_side_effects=True, vmem_limit_bytes=52 * 1024 * 1024),
         cost_estimate=pl.CostEstimate(
             flops=2 * rows * j_own * v * b * occ * c_own,
             bytes_accessed=2 * amplitudes.size, transcendentals=0),

time: 83 us -> 82.5 us (level)
  Pallas kernels: 80.9 us -> 79.8 us
    pallas_call x1, Pallas kernels: 80.9 us -> 79.8 us  [body(): pl.pallas_call(functools.partial(kernel, n, nw), out_shape=jax.ShapeDtype...]
    unnamed x1 -> x5, local copies, waits for them, and re-layouts: 1.88 us -> 2.52 us
where the time goes in v4:
time: 82.5 us; the launch traced here: 82.4 us
  Pallas kernels  79.8 us (97%)
  local copies, waits for them, and re-layouts  2.52 us (3%)
    pallas_call x1, Pallas kernels, body(): pl.pallas_call(functools.partial(kernel, n, nw), out_shape=jax.ShapeDtype...  79.8 us
    unnamed x5, local copies, waits for them, and re-layouts  2.52 us

profile of v4, /device:TPU:0, one launch (start us, length us, event | category | flops | bytes accessed | tf_op | source)
XLA Modules:
  0.0 82.4 jit_solution(7538679961933779382)
XLA Ops:
  0.0 0.0 copy-start
  0.0 1.0 %copy-done = bf16[4,8,32,256]{3,2,1,0:T(8,128)(2,1)S(1)} copy-done((bf16[4,8,32,256]{3,2,1,0:T(8,128)(2,1)S(1)}, bf16[4,8,32,256]{3,2,1,0:T(8,128)(2,1)}, u32[]{:S(2)}) %copy-start) | copy-done | bytes 524312
  1.0 0.0 copy-start.1
  1.0 0.7 copy-done.1
  1.7 79.8 %shard_map.37 = bf16[4,4,64,256]{3,2,1,0:T(8,128)(2,1)S(1)} custom-call(s32[4,32]{1,0:T(4,128)S(1)} %copy-done.1, bf16[4,8,32,256]{3,2,1,0:T(8,128)(2,1)S(1)} %copy-done, bf16[32,4,64,256]{3,2,1,0:T(8,128)(2,1)} %t_hbm.1), custom_call_target="tpu_custom_call" | custom-call | flops 4294967296 | bytes 4194304 | tf_op jit(solution)/shard_map/pallas_call | solution.py:280
  81.6 0.8 copy.5
Async XLA Ops:
  0.0 1.0 %copy-start = (bf16[4,8,32,256]{3,2,1,0:T(8,128)(2,1)S(1)}, bf16[4,8,32,256]{3,2,1,0:T(8,128)(2,1)}, u32[]{:S(2)}) copy-start(bf16[4,8,32,256]{3,2,1,0:T(8,128)(2,1)} %w_ref.1) | copy-start | bytes 1572868
  1.0 0.7 copy-start.1

commit v5 on v4

--- a/solution.py
+++ b/solution.py
@@ -10,33 +10,41 @@
 MESH = pl.DeviceIdType.MESH
 
 
-STEPS = 127.0 * 256.0
+LEVELS = 32767.0 * 16.0
 
 
 def encode(x):
-    head = x.astype(jnp.bfloat16)
-    wide = head.astype(jnp.float32)
-    zero = wide == 0.0
-    ratio = jnp.where(zero, 0.0, (x - wide) / jnp.where(zero, 1.0, wide))
-    steps = jnp.round(ratio * STEPS)
-    half = x.shape[0] // 2
-    tail = steps[:half] * 256.0 + (steps[half:] + 128.0)
-    return head, tail.astype(jnp.int32).astype(jnp.int16)
-
-
-def decode(head, tail):
-    both = tail.astype(jnp.int32).astype(jnp.float32)
-    upper = jnp.floor(both * (1.0 / 256.0))
-    lower = both - upper * 256.0 - 128.0
-    wide = head.astype(jnp.float32)
-    half = head.shape[0] // 2
-    return (wide[:half] + wide[:half] * (upper * (1.0 / STEPS)),
-            wide[half:] + wide[half:] * (lower * (1.0 / STEPS)))
-
-
-def kernel(n, nw, pairs, w_ref, t_hbm, out, src, t_ref, gath, part, head_out, tail_out, head_in, tail_in,
+    top = jnp.max(jnp.abs(x), axis=(0, 1), keepdims=True)
+    zero = top == 0.0
+    inverse = jnp.where(zero, 0.0, 1.0 / jnp.where(zero, 1.0, top))
+    level = jnp.round(x * inverse * LEVELS)
+    head = jnp.floor(level * (1.0 / 16.0) + 0.5)
+    low = level - head * 16.0 + 8.0
+    part = x.shape[0] // 4
+    tail = (low[:part] * 4096.0 + low[part:2 * part] * 256.0
+            + low[2 * part:3 * part] * 16.0 + low[3 * part:] - 32768.0)
+    return head.astype(jnp.int32).astype(jnp.int16), tail.astype(jnp.int32).astype(jnp.int16), top[0]
+
+
+def decode(head, tail, top):
+    rest = tail.astype(jnp.int32).astype(jnp.float32) + 32768.0
+    lows = []
+    for unit in (4096.0, 256.0, 16.0):
+        digit = jnp.floor(rest * (1.0 / unit))
+        lows.append(digit)
+        rest = rest - digit * unit
+    lows.append(rest)
+    part = head.shape[0] // 4
+    values = []
+    for q, low in enumerate(lows):
+        high = head[q * part:(q + 1) * part].astype(jnp.int32).astype(jnp.float32)
+        values.append((high * 16.0 + (low - 8.0)) * (1.0 / LEVELS) * top[None])
+    return values
+
+
+def kernel(n, nw, pairs, w_ref, t_hbm, out, src, t_ref, gath, part, head_out, tail_out, top_out, head_in, tail_in, top_in,
            t_sem, a2a_send, a2a_recv, xy_send, xy_recv, sib_send, sib_recv,
-           head_send, head_recv, tail_send, tail_recv):
+           head_send, head_recv, tail_send, tail_recv, top_send, top_recv):
     g, w = lax.axis_index("grp"), lax.axis_index("wide")
     chip, core = w // 2, w % 2
     chips = nw // 2
@@ -46,7 +54,7 @@
     split = chunks // rows
     lag = 2 * split
     c_own = v // n
-    half = t_ref.shape[1] // 2
+    quarter = t_ref.shape[1] // 4
     depth = k_here * c_own
 
     t_copy = pltpu.make_async_copy(t_hbm, t_ref, t_sem)
@@ -102,20 +110,21 @@
                     send_sem=sent.at[way, i, dest], recv_sem=came.at[way, i, dest],
                     device_id=to, device_id_type=MESH)
                 for box, slot, sent, came in (
-                    (head_out, head_in, head_send, head_recv), (tail_out, tail_in, tail_send, tail_recv))]
+                    (head_out, head_in, head_send, head_recv), (tail_out, tail_in, tail_send, tail_recv),
+                    (top_out, top_in, top_send, top_recv))]
 
         def start(self):
-            head_out[self.at], tail_out[self.at] = encode(part[self.at])
+            head_out[self.at], tail_out[self.at], top_out[self.at] = encode(part[self.at])
             for copy in self.copies:
                 copy.start()
 
         def add(self):
             for copy in self.copies:
                 copy.wait_recv()
-            low, high = decode(head_in[self.into], tail_in[self.into])
             i, dest = self.at
-            part[i, dest, :half] += low
-            part[i, dest, half:] += high
+            values = decode(head_in[self.into], tail_in[self.into], top_in[self.into])
+            for q, value in enumerate(values):
+                part[i, dest, q * quarter:(q + 1) * quarter] += value
 
         def wait_send(self):
             for copy in self.copies:
@@ -288,19 +297,22 @@
             pltpu.VMEM(amplitudes.shape, jnp.bfloat16),
             pltpu.VMEM((chunks, nw, a_c, n * k_own * c_own), jnp.bfloat16),
             pltpu.VMEM((chunks, n, j_own, a_out_c, b), jnp.float32),
-            pltpu.VMEM((chunks, n, j_own, a_out_c, b), jnp.bfloat16),
-            pltpu.VMEM((chunks, n, j_own // 2, a_out_c, b), jnp.int16),
-            pltpu.VMEM((2, chunks, n, j_own, a_out_c, b), jnp.bfloat16),
-            pltpu.VMEM((2, chunks, n, j_own // 2, a_out_c, b), jnp.int16),
+            pltpu.VMEM((chunks, n, j_own, a_out_c, b), jnp.int16),
+            pltpu.VMEM((chunks, n, j_own // 4, a_out_c, b), jnp.int16),
+            pltpu.VMEM((chunks, n, 1, b), jnp.float32),
+            pltpu.VMEM((2, chunks, n, j_own, a_out_c, b), jnp.int16),
+            pltpu.VMEM((2, chunks, n, j_own // 4, a_out_c, b), jnp.int16),
+            pltpu.VMEM((2, chunks, n, 1, b), jnp.float32),
             dma,
             dma((chunks, n)), dma((chunks, n)),
             dma((chunks, chips)), dma((chunks, chips)),
             dma((chunks, chips)), dma((chunks, chips)),
             dma((2, chunks, n)), dma((2, chunks, n)),
             dma((2, chunks, n)), dma((2, chunks, n)),
+            dma((2, chunks, n)), dma((2, chunks, n)),
         ],
         compiler_params=pltpu.CompilerParams(
-            collective_id=0, has_side_effects=True, vmem_limit_bytes=52 * 1024 * 1024),
+            collective_id=0, has_side_effects=True, vmem_limit_bytes=58 * 1024 * 1024),
         cost_estimate=pl.CostEstimate(
             flops=2 * rows * j_own * v * b * occ * c_own,
             bytes_accessed=2 * amplitudes.size, transcendentals=0),

time: 82.5 us -> 81.7 us (level)
    unnamed x5 -> x1, local copies, waits for them, and re-layouts: 2.52 us -> 1.88 us
where the time goes in v5:
time: 81.7 us; the launch traced here: 81.6 us
  Pallas kernels  79.7 us (98%)
  local copies, waits for them, and re-layouts  1.88 us (2%)
    pallas_call x1, Pallas kernels, body(): pl.pallas_call(functools.partial(kernel, n, nw), out_shape=jax.ShapeDtype...  79.7 us
    unnamed x1, local copies, waits for them, and re-layouts  1.88 us

profile of v5, /device:TPU:0, one launch (start us, length us, event | category | flops | bytes accessed | tf_op | source)
XLA Modules:
  0.0 81.6 jit_solution(2185201356852644039)
XLA Ops:
  0.0 79.7 %shard_map.37 = bf16[4,4,64,256]{3,2,1,0:T(8,128)(2,1)} custom-call(s32[4,32]{1,0:T(4,128)} %pairs.1, bf16[4,8,32,256]{3,2,1,0:T(8,128)(2,1)} %w_ref.1, bf16[32,4,64,256]{3,2,1,0:T(8,128)(2,1)} %t_hbm.1), custom_call_target="tpu_custom_call" | custom-call | flops 4294967296 | bytes 4194304 | tf_op jit(solution)/shard_map/pallas_call | solution.py:289
  79.7 1.9 %copy.5 = bf16[4,4,64,256]{3,2,1,0:T(8,128)(2,1)} copy(bf16[4,4,64,256]{3,2,1,0:T(8,128)(2,1)} %shard_map.37) | data formatting | bytes 1048576

commit v6 on v5

--- a/solution.py
+++ b/solution.py
@@ -222,26 +222,38 @@
                 at = pl.ds(pl.multiple_of(p * a_own + (i % split) * a_c, a_c), a_c)
                 out[i // split, :, at] = part[i, g, :, p * a_c:(p + 1) * a_c].astype(out.dtype)
 
+    def ahead(i):
+        @pl.when(i + 1 < chunks)
+        def _():
+            spread(i + 1)
+
+        @pl.when(i + 2 < chunks)
+        def _():
+            forward(i + 2)
+
     forward(0)
 
     @pl.loop(1, chunks)
     def _(i):
         exchange(i)
 
+    spread(0)
+    if chunks > 1:
+        forward(1)
+    t_copy.wait()
+
     @pl.loop(0, chunks)
     def _(i):
-        spread(i)
-
-        @pl.when(i + 1 < chunks)
-        def _():
-            forward(i + 1)
-
-        @pl.when(i == 0)
-        def _():
-            t_copy.wait()
+        @pl.when(i > 0)
+        def _():
+            ahead(i)
 
         compute(i)
         sources(i)
+
+        @pl.when(i == 0)
+        def _():
+            ahead(i)
 
         @pl.when(i > 0)
         def _():

time: 81.7 us -> 80.6 us (0.987)
  Pallas kernels: 79.7 us -> 78.5 us
    pallas_call x1, Pallas kernels: 79.7 us -> 78.5 us  [body(): pl.pallas_call(functools.partial(kernel, n, nw), out_shape=jax.ShapeDtype...]
where the time goes in v6:
time: 80.6 us; the launch traced here: 80.4 us
  Pallas kernels  78.5 us (97%)
  local copies, waits for them, and re-layouts  1.88 us (2%)
    pallas_call x1, Pallas kernels, body(): pl.pallas_call(functools.partial(kernel, n, nw), out_shape=jax.ShapeDtype...  78.5 us
    unnamed x1, local copies, waits for them, and re-layouts  1.88 us

profile of v6, /device:TPU:0, one launch (start us, length us, event | category | flops | bytes accessed | tf_op | source)
XLA Modules:
  0.0 80.4 jit_solution(11756813925482949158)
XLA Ops:
  0.0 78.5 %shard_map.37 = bf16[4,4,64,256]{3,2,1,0:T(8,128)(2,1)} custom-call(s32[4,32]{1,0:T(4,128)} %pairs.1, bf16[4,8,32,256]{3,2,1,0:T(8,128)(2,1)} %w_ref.1, bf16[32,4,64,256]{3,2,1,0:T(8,128)(2,1)} %t_hbm.1), custom_call_target="tpu_custom_call" | custom-call | flops 4294967296 | bytes 4194304 | tf_op jit(solution)/shard_map/pallas_call | solution.py:301
  78.5 1.9 %copy.5 = bf16[4,4,64,256]{3,2,1,0:T(8,128)(2,1)} copy(bf16[4,4,64,256]{3,2,1,0:T(8,128)(2,1)} %shard_map.37) | data formatting | bytes 1048576

commit v7 on v6

--- a/solution.py
+++ b/solution.py
@@ -52,7 +52,7 @@
     rows, k_here, a_own, v = w_ref.shape
     chunks, a_c = src.shape[1], src.shape[2]
     split = chunks // rows
-    lag = 2 * split
+    lag = chunks
     c_own = v // n
     quarter = t_ref.shape[1] // 4
     depth = k_here * c_own

time: 80.6 us -> 80.5 us (level)
  no operation moved by 1% of the time
where the time goes in v7:
time: 80.5 us; the launch traced here: 80.3 us
  Pallas kernels  78.4 us (97%)
  local copies, waits for them, and re-layouts  1.88 us (2%)
    pallas_call x1, Pallas kernels, body(): pl.pallas_call(functools.partial(kernel, n, nw), out_shape=jax.ShapeDtype...  78.4 us
    unnamed x1, local copies, waits for them, and re-layouts  1.88 us

profile of v7, /device:TPU:0, one launch (start us, length us, event | category | flops | bytes accessed | tf_op | source)
XLA Modules:
  0.0 80.3 jit_solution(3566302486575108295)
XLA Ops:
  0.0 78.4 %shard_map.37 = bf16[4,4,64,256]{3,2,1,0:T(8,128)(2,1)} custom-call(s32[4,32]{1,0:T(4,128)} %pairs.1, bf16[4,8,32,256]{3,2,1,0:T(8,128)(2,1)} %w_ref.1, bf16[32,4,64,256]{3,2,1,0:T(8,128)(2,1)} %t_hbm.1), custom_call_target="tpu_custom_call" | custom-call | flops 4294967296 | bytes 4194304 | tf_op jit(solution)/shard_map/pallas_call | solution.py:301
  78.5 1.9 %copy.5 = bf16[4,4,64,256]{3,2,1,0:T(8,128)(2,1)} copy(bf16[4,4,64,256]{3,2,1,0:T(8,128)(2,1)} %shard_map.37) | data formatting | bytes 1048576

commit v8 on v7

--- a/solution.py
+++ b/solution.py
@@ -295,7 +295,7 @@
     occ, j_own, _, b = amplitudes.shape
     a_out = a_own * nw // n
     chips = nw // 2
-    split = 2 if a_own % 32 == 0 else 1
+    split = 1
     chunks, a_c, a_out_c = rows * split, a_own // split, a_out // split
     dma = pltpu.SemaphoreType.DMA
     return pl.pallas_call(

time: 80.5 us -> 75.8 us (0.942)
  Pallas kernels: 78.4 us -> 73.8 us
    pallas_call x1, Pallas kernels: 78.4 us -> 73.8 us  [body(): pl.pallas_call(functools.partial(kernel, n, nw), out_shape=jax.ShapeDtype...]
where the time goes in v8:
time: 75.8 us; the launch traced here: 75.7 us
  Pallas kernels  73.8 us (97%)
  local copies, waits for them, and re-layouts  1.88 us (2%)
    pallas_call x1, Pallas kernels, body(): pl.pallas_call(functools.partial(kernel, n, nw), out_shape=jax.ShapeDtype...  73.8 us
    unnamed x1, local copies, waits for them, and re-layouts  1.88 us

profile of v8, /device:TPU:0, one launch (start us, length us, event | category | flops | bytes accessed | tf_op | source)
XLA Modules:
  0.0 75.7 jit_solution(7655800304467671129)
XLA Ops:
  0.0 73.8 %shard_map.37 = bf16[4,4,64,256]{3,2,1,0:T(8,128)(2,1)} custom-call(s32[4,32]{1,0:T(4,128)} %pairs.1, bf16[4,8,32,256]{3,2,1,0:T(8,128)(2,1)} %w_ref.1, bf16[32,4,64,256]{3,2,1,0:T(8,128)(2,1)} %t_hbm.1), custom_call_target="tpu_custom_call" | custom-call | flops 4294967296 | bytes 4194304 | tf_op jit(solution)/shard_map/pallas_call | solution.py:301
  73.8 1.9 %copy.5 = bf16[4,4,64,256]{3,2,1,0:T(8,128)(2,1)} copy(bf16[4,4,64,256]{3,2,1,0:T(8,128)(2,1)} %shard_map.37) | data formatting | bytes 1048576
